TPU v7x, 256 devices: a whole 4x4x8 slice. The times are simulated.
256 devices in a mesh: band: 8 (over y, x_lo), grow: 32 (over x_hi, z, core).
Axes of the slice: x: 4 (x_hi: 2, x_lo: 2; x = x_hi * 2 + x_lo), y: 4, z: 8, core: 2. Of those that a mesh axis runs over, the one named last changes fastest.
Arguments:
- pair_matrices: bfloat16 [16, 64, 15360], P(None, 'band', 'grow')
- screened: bfloat16 [15360, 15360], P('grow', 'band'), as said below
Outputs:
- sigma: float32 [16, 16], replicated
Inputs may be any that keep to these rules, and one draw needn't show every extreme that they name: screened is symmetric.
All inputs are finite; a program needn't handle non-finite values.
Results may differ from a plain program's by a relative error of at most 0.0003.
Values may be sent and summed in bfloat16 or wider, within the bound.
A program may use at most 192 MiB of HBM per device.

v0:
```python
import jax
import jax.numpy as jnp
from jax import lax
from jax.sharding import PartitionSpec as P


def from_behind(x, axis, by):
    devices = lax.axis_size(axis)
    return lax.ppermute(x, axis, [(i, (i + by) % devices) for i in range(devices)])


def body(pair_matrices, screened):
    states, band_local, grow_local = pair_matrices.shape
    panel_width = screened.shape[1]
    cycle_size = lax.axis_size("band")
    position = lax.axis_index("band")
    gathered = lax.all_gather(pair_matrices, "grow", axis=2, tiled=True)
    flat_rows = pair_matrices.reshape(states * band_local, grow_local)

    def contribute(sigma_sum, w_panel, anchor):
        partial_x = jnp.dot(flat_rows, w_panel, preferred_element_type=jnp.float32)
        partial_x = partial_x.reshape(states, band_local, panel_width)
        columns = lax.dynamic_slice_in_dim(gathered, anchor * panel_width, panel_width, 2).astype(
            jnp.float32
        )
        return sigma_sum + jnp.einsum(
            "sbh,tbh->st", partial_x, columns, precision=lax.Precision.HIGHEST
        )

    sigma_sum = jnp.zeros((states, states), jnp.float32)
    sigma_sum = contribute(sigma_sum, screened, position)
    w_panel = screened
    for shift_step in range(1, cycle_size):
        w_panel = from_behind(w_panel, "band", 1)
        sigma_sum = contribute(sigma_sum, w_panel, (position - shift_step) % cycle_size)
    sigma_sum = -sigma_sum
    sigma_sum = lax.psum(sigma_sum, ("band", "grow"))
    return sigma_sum


def solution(mesh):
    placed = (P(None, "band", "grow"), P("grow", "band"))
    return jax.shard_map(body, mesh=mesh, in_specs=placed, out_specs=P(), check_vma=False)
```

profile of v0, /device:TPU:1, one launch (start us, length us, event | category | flops | bytes accessed | tf_op | source)
XLA Modules:
  0.0 477.8 jit_solution(8546091767634625740)
XLA Ops:
  6.5 2.0 collective-permute-start
  8.6 2.6 copy.4
  11.2 48.5 %collective-permute-done = bf16[480,1920]{1,0:T(8,128)(2,1)S(1)} collective-permute-done((bf16[480,1920]{1,0:T(8,128)(2,1)}, bf16[480,1920]{1,0:T(8,128)(2,1)S(1)}, u32[]{:S(2)}, u32[]{:S(2)}) %collective-permute-start) | collective-permute-done | bytes 1843232 | tf_op jit(solution)/shard_map/ppermute | solution.py:9
  59.7 0.5 collective-permute-start.1
  60.2 42.8 %collective-permute-done.1 = bf16[480,1920]{1,0:T(8,128)(2,1)S(1)} collective-permute-done((bf16[480,1920]{1,0:T(8,128)(2,1)S(1)}, bf16[480,1920]{1,0:T(8,128)(2,1)S(1)}, u32[]{:S(2)}, u32[]{:S(2)}) %collective-permute-start.1) | collective-permute-done | bytes 1843232 | tf_op jit(solution)/shard_map/ppermute | solution.py:9
  103.0 1.2 copy-done.7
  104.2 3.8 collective-permute-start.2
  108.0 79.9 %collective-permute-done.2 = bf16[480,1920]{1,0:T(8,128)(2,1)S(1)} collective-permute-done((bf16[480,1920]{1,0:T(8,128)(2,1)S(1)}, bf16[480,1920]{1,0:T(8,128)(2,1)S(1)}, u32[]{:S(2)}, u32[]{:S(2)}) %collective-permute-start.2) | collective-permute-done | bytes 1843232 | tf_op jit(solution)/shard_map/ppermute | solution.py:9
  187.9 1.2 copy-done.9
  189.1 0.9 collective-permute-start.3
  190.0 73.8 %collective-permute-done.3 = bf16[480,1920]{1,0:T(8,128)(2,1)} collective-permute-done((bf16[480,1920]{1,0:T(8,128)(2,1)S(1)}, bf16[480,1920]{1,0:T(8,128)(2,1)}, u32[]{:S(2)}, u32[]{:S(2)}) %collective-permute-start.3) | collective-permute-done | bytes 1843232 | tf_op jit(solution)/shard_map/ppermute | solution.py:9
  263.8 3.2 fusion.30
  267.0 1.4 fusion.28
  268.9 0.4 fusion.24
  269.3 2.0 fusion.22
  271.3 32.6 %collective-permute-done.4 = bf16[480,1920]{1,0:T(8,128)(2,1)} collective-permute-done((bf16[480,1920]{1,0:T(8,128)(2,1)}, bf16[480,1920]{1,0:T(8,128)(2,1)}, u32[]{:S(2)}, u32[]{:S(2)}) %collective-permute-start.4) | collective-permute-done | bytes 1843232 | tf_op jit(solution)/shard_map/ppermute | solution.py:9
  303.9 13.3 %all-gather.2.cloned.1.call-done = bf16[16,8,15360]{0,1,2:T(8,128)(2,1)} async-done(((bf16[16,8,480]{0,1,2:T(8,128)(2,1)}), bf16[16,8,15360]{0,1,2:T(8,128)(2,1)}) %all-gather.2.cloned.1.call-update) | async-done | bytes 3932176 | tf_op jit(solution)/shard_map/all_gather | solution.py:17
  317.3 18.8 %constant_dynamic-slice_fusion = (bf16[16,8,1920]{0,1,2:T(8,128)(2,1)S(1)}, bf16[16,8,1920]{0,1,2:T(8,128)(2,1)S(1)}, bf16[16,8,1920]{0,1,2:T(8,128)(2,1)}, bf16...) fusion(bf16[16,8,15360]{0,1,2:T(8,128)(2,1)} %all-gather.2.clon, ...), kind=kLoop, calls=%fused_computation.56 | loop fusion | bytes 7864352 | tf_op jit(solution)/shard_map/dynamic_slice | solution.py:23
  336.1 4.8 %fusion.32 = f32[16,16]{1,0:T(8,128)S(1)} fusion(f32[16,8,1920]{2,0,1:T(8,128)} %fusion.30, bf16[16,8,1920]{0,1,2:T(8,128)(2,1)} %get-tuple-element.12), kind=kOutput, calls=%fused_computation.32 | convolution fusion | flops 47185920 | bytes 1475584 | tf_op jit(solution)/shard_map/sbh,tbh->st/dot_general | solution.py:26
  340.9 2.2 fusion.77
  343.1 2.2 fusion.74
  345.4 2.5 collective-permute-start.6
  347.9 2.2 fusion.71
  350.1 2.2 fusion.68
  352.3 2.0 fusion.20
  354.3 2.2 fusion.65
  356.4 1.9 fusion.18
  358.4 2.2 fusion.62
  360.6 26.3 %collective-permute-done.6 = bf16[480,1920]{1,0:T(8,128)(2,1)S(1)} collective-permute-done((bf16[480,1920]{1,0:T(8,128)(2,1)}, bf16[480,1920]{1,0:T(8,128)(2,1)S(1)}, u32[]{:S(2)}, u32[]{:S(2)}) %collective-permute-start.6) | collective-permute-done | bytes 1843232 | tf_op jit(solution)/shard_map/ppermute | solution.py:9
  386.9 0.5 fusion.16
  387.4 2.2 fusion.59
  389.5 81.4 %psum.7 = f32[16,16]{1,0:T(8,128)} all-reduce(f32[16,16]{1,0:T(8,128)S(1)} %fusion.59), channel_id=1, replica_groups=mesh['band'=8,'grow'=32] {'band','grow'}, use_global_device_ids=true, to_apply=%region_0.1 | all-reduce | flops 256 | bytes 2048 | tf_op jit(solution)/shard_map/psum | solution.py:37
  (26 shorter events, 0.5 us)
Async XLA Ops:
  6.5 260.5 %copy-start.5 = (bf16[16,8,480]{2,1,0:T(8,128)(2,1)S(1)}, bf16[16,8,480]{2,1,0:T(8,128)(2,1)}, u32[]{:S(2)}) copy-start(bf16[16,8,480]{2,1,0:T(8,128)(2,1)} %param.2) | copy-start | bytes 368644
  6.5 310.7 %all-gather.2.cloned.1.call-start = ((), (), s32[]{:S(2)}) async-start(), calls=%async_computation | async-start | bytes 32440320 | tf_op jit(solution)/shard_map/all_gather | solution.py:17
  6.5 53.1 %collective-permute-start = (bf16[480,1920]{1,0:T(8,128)(2,1)}, bf16[480,1920]{1,0:T(8,128)(2,1)S(1)}, u32[]{:S(2)}, u32[]{:S(2)}) collective-permute-start(bf16[480,1920]{1,0:T(8,128)(2,1)} %param.3), channel_id=1, source_target_pairs={{0,32},{32,64},{64,96},{96,128},{128,160},{160,192},{192,224},{224... | collective-permute-start | bytes 5529608 | tf_op jit(solution)/shard_map/ppermute | solution.py:9
  59.7 43.3 %collective-permute-start.1 = (bf16[480,1920]{1,0:T(8,128)(2,1)S(1)}, bf16[480,1920]{1,0:T(8,128)(2,1)S(1)}, u32[]{:S(2)}, u32[]{:S(2)}) collective-permute-start(bf16[480,1920]{1,0:T(8,128)(2,1)S(1)} %collective-permute-done), channel_id=1, source_target_pairs={{0,32},{32,64},{64,96},{96,128},{128,160},{160,192},{192,224},{224... | collective-permute-start | bytes 5529608 | tf_op jit(solution)/shard_map/ppermute | solution.py:9
  103.0 1.2 copy-start.7
  104.2 83.7 %collective-permute-start.2 = (bf16[480,1920]{1,0:T(8,128)(2,1)S(1)}, bf16[480,1920]{1,0:T(8,128)(2,1)S(1)}, u32[]{:S(2)}, u32[]{:S(2)}) collective-permute-start(bf16[480,1920]{1,0:T(8,128)(2,1)S(1)} %collective-permute-done.1), channel_id=1, source_target_pairs={{0,32},{32,64},{64,96},{96,128},{128,160},{160,192},{192,224},{224... | collective-permute-start | bytes 5529608 | tf_op jit(solution)/shard_map/ppermute | solution.py:9
  187.9 1.2 copy-start.9
  189.1 74.6 %collective-permute-start.3 = (bf16[480,1920]{1,0:T(8,128)(2,1)S(1)}, bf16[480,1920]{1,0:T(8,128)(2,1)}, u32[]{:S(2)}, u32[]{:S(2)}) collective-permute-start(bf16[480,1920]{1,0:T(8,128)(2,1)S(1)} %collective-permute-done.2), channel_id=1, source_target_pairs={{0,32},{32,64},{64,96},{96,128},{128,160},{160,192},{192,224},{224... | collective-permute-start | bytes 5529608 | tf_op jit(solution)/shard_map/ppermute | solution.py:9
  263.8 40.1 %collective-permute-start.4 = (bf16[480,1920]{1,0:T(8,128)(2,1)}, bf16[480,1920]{1,0:T(8,128)(2,1)}, u32[]{:S(2)}, u32[]{:S(2)}) collective-permute-start(bf16[480,1920]{1,0:T(8,128)(2,1)} %collective-permute-done.3), channel_id=1, source_target_pairs={{0,32},{32,64},{64,96},{96,128},{128,160},{160,192},{192,224},{224... | collective-permute-start | bytes 5529608 | tf_op jit(solution)/shard_map/ppermute | solution.py:9
  263.8 4.6 copy-start.8
  263.8 5.1 %copy-start.10 = (bf16[480,1920]{1,0:T(8,128)(2,1)S(1)}, bf16[480,1920]{1,0:T(8,128)(2,1)}, u32[]{:S(2)}) copy-start(bf16[480,1920]{1,0:T(8,128)(2,1)} %copy-done.9) | copy-start | bytes 5529604
  303.9 41.5 %collective-permute-start.5 = (bf16[480,1920]{1,0:T(8,128)(2,1)}, bf16[480,1920]{1,0:T(8,128)(2,1)}, u32[]{:S(2)}, u32[]{:S(2)}) collective-permute-start(bf16[480,1920]{1,0:T(8,128)(2,1)} %collective-permute-done.4), channel_id=1, source_target_pairs={{0,32},{32,64},{64,96},{96,128},{128,160},{160,192},{192,224},{224... | collective-permute-start | bytes 5529608 | tf_op jit(solution)/shard_map/ppermute | solution.py:9
  336.0 4.8 %copy-start.4 = (bf16[16,8,1920]{0,1,2:T(8,128)(2,1)S(1)}, bf16[16,8,1920]{0,1,2:T(8,128)(2,1)}, u32[]{:S(2)}) copy-start(bf16[16,8,1920]{0,1,2:T(8,128)(2,1)} %get-tuple-element.11) | copy-start | bytes 1474564
  336.0 4.8 %copy-start.6 = (f32[16,8,1920]{2,0,1:T(8,128)S(1)}, f32[16,8,1920]{2,0,1:T(8,128)}, u32[]{:S(2)}) copy-start(f32[16,8,1920]{2,0,1:T(8,128)} %fusion.28) | copy-start | bytes 2949124
  336.1 7.1 %copy-start.3 = (bf16[16,8,1920]{0,1,2:T(8,128)(2,1)S(1)}, bf16[16,8,1920]{0,1,2:T(8,128)(2,1)}, u32[]{:S(2)}) copy-start(bf16[16,8,1920]{0,1,2:T(8,128)(2,1)} %get-tuple-element.10) | copy-start | bytes 1474564
  340.9 7.0 %copy-start.2 = (bf16[16,8,1920]{0,1,2:T(8,128)(2,1)S(1)}, bf16[16,8,1920]{0,1,2:T(8,128)(2,1)}, u32[]{:S(2)}) copy-start(bf16[16,8,1920]{0,1,2:T(8,128)(2,1)} %get-tuple-element.9) | copy-start | bytes 1474564
  343.1 6.9 %copy-start.1 = (bf16[16,8,1920]{0,1,2:T(8,128)(2,1)S(1)}, bf16[16,8,1920]{0,1,2:T(8,128)(2,1)}, u32[]{:S(2)}) copy-start(bf16[16,8,1920]{0,1,2:T(8,128)(2,1)} %get-tuple-element.8) | copy-start | bytes 1474564
  345.4 41.5 %collective-permute-start.6 = (bf16[480,1920]{1,0:T(8,128)(2,1)}, bf16[480,1920]{1,0:T(8,128)(2,1)S(1)}, u32[]{:S(2)}, u32[]{:S(2)}) collective-permute-start(bf16[480,1920]{1,0:T(8,128)(2,1)} %collective-permute-done.5), channel_id=1, source_target_pairs={{0,32},{32,64},{64,96},{96,128},{128,160},{160,192},{192,224},{224... | collective-permute-start | bytes 5529608 | tf_op jit(solution)/shard_map/ppermute | solution.py:9
  350.1 4.2 copy-start
Sparse Core Ops, SparseCore 0:
  11.3 305.8 all-gather.1
where the time goes:
time: 478 us
  waiting for transfers between devices  317 us (66%)
  blocking collectives  81.4 us (17%)
  matrix products  32 us (7%)
  local copies, waits for them, and re-layouts  23.9 us (5%)
  between operations  13.6 us (3%)
  starting transfers between devices  9.72 us (2%)
    ppermute x7, waiting for transfers between devices, from_behind(): lax.ppermute(x, axis, [(i, (i + by) % devices) for i in range(devices)])  304 us
    psum x1, blocking collectives, body(): sigma_sum = lax.psum(sigma_sum, ('band', 'grow'))  81.4 us
    dot_general x8, matrix products, contribute(): jnp.einsum('sbh,tbh->st', partial_x, columns, precision=lax.Precision.HIG...  20.2 us
    dynamic_slice x1, local copies, waits for them, and re-layouts, contribute(): lax.dynamic_slice_in_dim(gathered, anchor * panel_width, panel_width, 2)  18.8 us
    all_gather x1, waiting for transfers between devices, body(): gathered = lax.all_gather(pair_matrices, 'grow', axis=2, tiled=True)  13.3 us
    dot_general x8, matrix products, contribute(): partial_x = jnp.dot(flat_rows, w_panel, preferred_element_type=jnp.float32)  11.9 us
    ppermute x7, starting transfers between devices, from_behind(): lax.ppermute(x, axis, [(i, (i + by) % devices) for i in range(devices)])  9.72 us
  transfers between devices with their start and end apart: 8, of which 7 were waited for; matrix products, arithmetic and copies ran while one was open for 11% of the time, Pallas kernels for 0%

commit v1 on v0

v1 whole, which is shorter than its diff:
```python
import functools

import jax
import jax.numpy as jnp
from jax import lax
from jax.experimental import pallas as pl
from jax.experimental.pallas import tpu as pltpu
from jax.sharding import PartitionSpec as P

MESH = pl.DeviceIdType.MESH


def half_of(a, b):
    odd = (a + b) % 2
    return jnp.where(odd == 1, a % 2, jnp.where(a > b, 1, 0))


def kernel(nb, m_hbm, w_hbm, out_ref, m_own, mt_own, w, rows, cols, gram, red1, red2,
           load_sem, row_send, row_recv, col_send, col_recv, fwd_send, red1_send, red1_recv, red2_send, red2_recv):
    p, q = lax.axis_index("band"), lax.axis_index("grow")
    core, chip = q % 2, q // 2
    line, side = chip // 2, chip % 2
    diag = line == p
    first = jnp.where(diag, side, half_of(line, p))
    n_rows, n_cols = m_own.shape
    n_chips = 2 * nb
    tile = mt_own.shape[0]

    load_m = pltpu.make_async_copy(m_hbm, m_own, load_sem.at[0])
    load_w = pltpu.make_async_copy(w_hbm, w, load_sem.at[1])
    load_m.start()
    load_w.start()

    def row_needed(p_to, chip_at, p_from):
        at = chip_at // 2
        return jnp.logical_or(at == p_to, half_of(at, p_to) == p_from % 2)

    def col_needed(p_at, chip_at, p_from, r):
        at = chip_at // 2
        here = chip_at % 2
        return jnp.where(at == p_at, jnp.logical_or(r // 2 == here, p_from % 2 == here), half_of(at, p_at) == p_from % 2)

    barrier = pltpu.get_barrier_semaphore()

    def greet(p_to, q_to):
        pl.semaphore_signal(barrier, inc=1, device_id=(p_to, q_to), device_id_type=MESH)

    def greet_columns(i, carry):
        p_from, r = i // 2, 2 * (i % 2) + core
        q_from = 4 * p + r

        @pl.when(jnp.logical_and(col_needed(p, chip, p_from, r), jnp.logical_or(p_from != p, q_from != q)))
        def _():
            greet(p_from, q_from)

        return carry

    lax.fori_loop(0, 2 * nb, greet_columns, 0)

    def greet_plane(i, carry):
        other = (2 * p + core + i) % (2 * nb)
        greet(other // 2, 2 * chip + other % 2)
        return carry

    lax.fori_loop(1, 2 * nb, greet_plane, 0)

    def greet_line(i, carry):
        greet(p, 2 * ((chip + i) % n_chips) + core)
        return carry

    lax.fori_loop(1, n_chips, greet_line, 0)

    load_m.wait()
    mt_own[...] = m_own[...].T

    def sends_column(chip_to):
        needed = col_needed(line, chip_to, p, q % 4)
        return jnp.logical_and(needed, jnp.logical_or(p != line, chip_to != chip))

    def count(i, total):
        return total + jnp.where(sends_column(i), 1, 0)

    n_columns = lax.fori_loop(0, n_chips, count, 0)
    pl.semaphore_wait(barrier, n_columns + (2 * nb - 1) + (n_chips - 1))

    def column_copy(chip_to):
        return pltpu.make_async_remote_copy(
            src_ref=mt_own, dst_ref=cols.at[p, q % 4], send_sem=col_send.at[chip_to], recv_sem=col_recv.at[p, q % 4],
            device_id=(line, 2 * chip_to + core), device_id_type=MESH)

    def row_copy(p_to):
        return pltpu.make_async_remote_copy(
            src_ref=m_own, dst_ref=rows.at[p], send_sem=row_send.at[p_to], recv_sem=row_recv.at[p],
            device_id=(p_to, q), device_id_type=MESH)

    def send_columns(i, carry):
        chip_to = (chip + i) % n_chips

        @pl.when(sends_column(chip_to))
        def _():
            column_copy(chip_to).start()

        return carry

    lax.fori_loop(0, n_chips, send_columns, 0)

    def sends_row(p_to):
        return jnp.logical_and(p_to != p, row_needed(p_to, chip, p))

    def send_rows(i, carry):
        p_to = (p + i) % nb

        @pl.when(sends_row(p_to))
        def _():
            row_copy(p_to).start()

        return carry

    lax.fori_loop(1, nb, send_rows, 0)

    rows[p] = m_own[...]
    load_w.wait()

    @pl.when(diag)
    def _():
        cols[p, q % 4] = mt_own[...]
        lane = lax.broadcasted_iota(jnp.int32, w.shape, 1)
        own_half = (lane >= side * 2 * tile) & (lane < (side + 1) * 2 * tile)
        w[...] = jnp.where(own_half, w[...] * jnp.bfloat16(0.5), w[...])

        def clear(k, carry):
            p_from = 2 * k + 1 - side
            for r in range(2):
                cols[p_from, 2 * (1 - side) + r] = jnp.zeros((tile, n_rows), jnp.bfloat16)
            return carry

        lax.fori_loop(0, nb // 2, clear, 0)

    gram[...] = jnp.zeros_like(gram)

    def forward(p_from, r):
        return pltpu.make_async_remote_copy(
            src_ref=cols.at[p_from, r], dst_ref=cols.at[p_from, r], send_sem=fwd_send.at[p_from, r],
            recv_sem=col_recv.at[p_from, r], device_id=(p, q + 1 - 2 * core), device_id_type=MESH)

    group = min(2, nb // 2)
    steps = (nb // 2) // group
    n_steps = jnp.where(diag, 2 * steps, steps)

    def band_of(step, j):
        half = jnp.where(step < steps, first, 1 - first)
        return 2 * ((step % steps) * group + j) + half

    def step_body(step, carry):
        for j in range(group):
            p_from = band_of(step, j)
            for k in range(2):
                r = 2 * k + core

                @pl.when(col_needed(p, chip, p_from, r))
                def _():
                    @pl.when(jnp.logical_or(p_from != p, 4 * p + r != q))
                    def _():
                        forward(p_from, r).wait_recv()

                    forward(p_from, r).start()

        for j in range(group):
            p_from = band_of(step, j)
            for k in range(2):
                r = 2 * k + 1 - core

                @pl.when(col_needed(p, chip, p_from, r))
                def _():
                    forward(p_from, r).wait_recv()

            @pl.when(p_from != p)
            def _():
                pltpu.make_async_remote_copy(
                    src_ref=m_own, dst_ref=rows.at[p_from], send_sem=row_send.at[p_from], recv_sem=row_recv.at[p_from],
                    device_id=(p_from, q), device_id_type=MESH).wait_recv()

        right = [cols[band_of(step, j)].reshape(4 * tile, n_rows) for j in range(group)]
        z = jnp.dot(w[...], jnp.concatenate(right, axis=1), preferred_element_type=jnp.float32)
        high = z.astype(jnp.bfloat16)
        low = (z - high.astype(jnp.float32)).astype(jnp.bfloat16)
        for j in range(group):
            part = slice(j * n_rows, (j + 1) * n_rows)
            both = jnp.concatenate([high[:, part], low[:, part]], axis=1)
            g = jnp.dot(rows[band_of(step, j)], both, preferred_element_type=jnp.float32)
            gram[...] += g[:, :n_rows] + g[:, n_rows:]
        return carry

    lax.fori_loop(0, n_steps, step_body, 0)

    bands = n_rows // 16
    row_id = lax.broadcasted_iota(jnp.int32, gram.shape, 0)
    lane_id = lax.broadcasted_iota(jnp.int32, gram.shape, 1)
    kept = jnp.where(row_id % bands == lane_id % bands, gram[...], 0.0)
    place1 = 2 * p + core
    red1[place1] = kept.reshape(16, bands, n_rows).sum(axis=1)

    def plane_copy(other):
        return pltpu.make_async_remote_copy(
            src_ref=red1.at[place1], dst_ref=red1.at[place1], send_sem=red1_send.at[other], recv_sem=red1_recv.at[place1],
            device_id=(other // 2, 2 * chip + other % 2), device_id_type=MESH)

    def plane_wait(other):
        pltpu.make_async_remote_copy(
            src_ref=red1.at[place1], dst_ref=red1.at[other], send_sem=red1_send.at[other], recv_sem=red1_recv.at[other],
            device_id=(other // 2, 2 * chip + other % 2), device_id_type=MESH).wait_recv()

    def line_copy(other):
        return pltpu.make_async_remote_copy(
            src_ref=red2.at[chip], dst_ref=red2.at[chip], send_sem=red2_send.at[other], recv_sem=red2_recv.at[chip],
            device_id=(p, 2 * other + core), device_id_type=MESH)

    def line_wait(other):
        pltpu.make_async_remote_copy(
            src_ref=red2.at[chip], dst_ref=red2.at[other], send_sem=red2_send.at[other], recv_sem=red2_recv.at[other],
            device_id=(p, 2 * other + core), device_id_type=MESH).wait_recv()

    def loop(lo, hi, act):
        def body(i, carry):
            act(i)
            return carry

        lax.fori_loop(lo, hi, body, 0)

    loop(1, 2 * nb, lambda i: plane_copy((place1 + i) % (2 * nb)).start())
    loop(1, 2 * nb, lambda i: plane_wait((place1 + i) % (2 * nb)))
    red2[chip] = red1[...].sum(axis=0)
    loop(1, n_chips, lambda i: line_copy((chip + i) % n_chips).start())
    loop(1, n_chips, lambda i: line_wait((chip + i) % n_chips))
    total = red2[...].sum(axis=0)
    fold = jnp.where(
        lax.broadcasted_iota(jnp.int32, (n_rows, 16), 0) // bands == lax.broadcasted_iota(jnp.int32, (n_rows, 16), 1), 1.0, 0.0)
    s = jnp.dot(total, fold, precision=lax.Precision.HIGHEST, preferred_element_type=jnp.float32)
    s_t = lax.dot_general(fold, total, (((0,), (1,)), ((), ())), precision=lax.Precision.HIGHEST,
                          preferred_element_type=jnp.float32)
    out_ref[...] = -(s + s_t)

    loop(1, 2 * nb, lambda i: plane_copy((place1 + i) % (2 * nb)).wait_send())
    loop(1, n_chips, lambda i: line_copy((chip + i) % n_chips).wait_send())

    def sent_column(i):
        @pl.when(sends_column(i))
        def _():
            column_copy(i).wait_send()

    def sent_row(i):
        @pl.when(sends_row(i))
        def _():
            row_copy(i).wait_send()

    def sent_forward(i):
        p_from, r = i // 2, 2 * (i % 2) + core

        @pl.when(col_needed(p, chip, p_from, r))
        def _():
            forward(p_from, r).wait_send()

    loop(0, n_chips, sent_column)
    loop(0, nb, sent_row)
    loop(0, 2 * nb, sent_forward)


def body(nb, pair_matrices, screened):
    states, bands, tile = pair_matrices.shape
    flat = pair_matrices.reshape(states * bands, tile)
    n = states * bands
    dma = pltpu.SemaphoreType.DMA
    return pl.pallas_call(
        functools.partial(kernel, nb),
        out_shape=jax.ShapeDtypeStruct((states, states), jnp.float32),
        in_specs=[pl.BlockSpec(memory_space=pl.ANY)] * 2,
        out_specs=pl.BlockSpec(memory_space=pltpu.VMEM),
        scratch_shapes=[
            pltpu.VMEM((n, tile), jnp.bfloat16),
            pltpu.VMEM((tile, n), jnp.bfloat16),
            pltpu.VMEM(screened.shape, jnp.bfloat16),
            pltpu.VMEM((nb, n, tile), jnp.bfloat16),
            pltpu.VMEM((nb, 4, tile, n), jnp.bfloat16),
            pltpu.VMEM((n, n), jnp.float32),
            pltpu.VMEM((2 * nb, states, n), jnp.float32),
            pltpu.VMEM((2 * nb, states, n), jnp.float32),
            dma((2,)), dma((nb,)), dma((nb,)), dma((2 * nb,)), dma((nb, 4)), dma((nb, 4)),
            dma((2 * nb,)), dma((2 * nb,)), dma((2 * nb,)), dma((2 * nb,)),
        ],
        compiler_params=pltpu.CompilerParams(collective_id=0, has_side_effects=True, vmem_limit_bytes=40 * 1024 * 1024),
    )(flat, screened)


def solution(mesh):
    placed = (P(None, "band", "grow"), P("grow", "band"))
    return jax.shard_map(functools.partial(body, mesh.shape["band"]), mesh=mesh, in_specs=placed, out_specs=P(), check_vma=False)
```

time: 478 us -> 79.2 us (0.17)
  waiting for transfers between devices: 317 us -> 0 us
  blocking collectives: 81.4 us -> 0 us
  Pallas kernels: 0 us -> 76 us
  matrix products: 32 us -> 0 us
  local copies, waits for them, and re-layouts: 23.9 us -> 3.01 us
  between operations: 13.6 us -> 0.01 us
  starting transfers between devices: 9.72 us -> 0 us
    ppermute x7 -> x0, waiting for transfers between devices: 304 us -> none  [from_behind(): lax.ppermute(x, axis, [(i, (i + by) % devices) for i in range(devices)])]
    psum x1 -> x0, blocking collectives: 81.4 us -> none  [body(): sigma_sum = lax.psum(sigma_sum, ('band', 'grow'))]
    pallas_call x0 -> x1, Pallas kernels: none -> 76 us  [body(): pl.pallas_call(functools.partial(kernel, nb), out_shape=jax.ShapeDtypeStr...]
    dot_general x16 -> x0, matrix products: 32 us -> none  [the longest x8 20.2 us: contribute(): jnp.einsum('sbh,tbh->st', partial_x, columns, precision=lax.Precision.HIG...]
    dynamic_slice x1 -> x0, local copies, waits for them, and re-layouts: 18.8 us -> none  [contribute(): lax.dynamic_slice_in_dim(gathered, anchor * panel_width, panel_width, 2)]
    all_gather x1 -> x0, waiting for transfers between devices: 13.3 us -> none  [body(): gathered = lax.all_gather(pair_matrices, 'grow', axis=2, tiled=True)]
    ppermute x7 -> x0, starting transfers between devices: 9.72 us -> none  [from_behind(): lax.ppermute(x, axis, [(i, (i + by) % devices) for i in range(devices)])]
  transfers between devices with their start and end apart: 8 -> 0, of which waited for: 7 -> 0; matrix products, arithmetic and copies ran while one was open for 11% -> 0% of each run, Pallas kernels for 0% -> 0%
where the time goes in v1:
time: 79.2 us; the launch traced here: 79.1 us
  Pallas kernels  76 us (96%)
  local copies, waits for them, and re-layouts  3.01 us (4%)
    pallas_call x1, Pallas kernels, body(): pl.pallas_call(functools.partial(kernel, nb), out_shape=jax.ShapeDtypeStr...  76 us
    unnamed x5, local copies, waits for them, and re-layouts  3.01 us

profile of v1, /device:TPU:1, one launch (start us, length us, event | category | flops | bytes accessed | tf_op | source)
XLA Modules:
  0.0 79.1 jit_solution(3268989467226948037)
XLA Ops:
  0.0 0.0 copy-start
  0.0 1.5 %copy-done = bf16[480,1920]{1,0:T(8,128)(2,1)S(1)} copy-done((bf16[480,1920]{1,0:T(8,128)(2,1)S(1)}, bf16[480,1920]{1,0:T(8,128)(2,1)}, u32[]{:S(2)}) %copy-start) | copy-done | bytes 1843224
  1.5 0.0 copy-start.1
  1.5 0.9 %copy-done.1 = bf16[16,8,480]{2,1,0:T(8,128)(2,1)S(1)} copy-done((bf16[16,8,480]{2,1,0:T(8,128)(2,1)S(1)}, bf16[16,8,480]{2,1,0:T(8,128)(2,1)}, u32[]{:S(2)}) %copy-start.1) | copy-done | bytes 122904
  2.4 76.0 %shard_map.28 = f32[16,16]{1,0:T(8,128)S(1)} custom-call(bf16[128,480]{1,0:T(8,128)(2,1)S(1)} %bitcast.1, bf16[480,1920]{1,0:T(8,128)(2,1)S(1)} %copy-done), custom_call_target="tpu_custom_call" | custom-call | tf_op jit(solution)/shard_map/pallas_call | solution.py:273
  78.5 0.6 copy.4
Async XLA Ops:
  0.0 1.5 %copy-start = (bf16[480,1920]{1,0:T(8,128)(2,1)S(1)}, bf16[480,1920]{1,0:T(8,128)(2,1)}, u32[]{:S(2)}) copy-start(bf16[480,1920]{1,0:T(8,128)(2,1)} %w_hbm.1) | copy-start | bytes 5529604
  1.5 0.9 %copy-start.1 = (bf16[16,8,480]{2,1,0:T(8,128)(2,1)S(1)}, bf16[16,8,480]{2,1,0:T(8,128)(2,1)}, u32[]{:S(2)}) copy-start(bf16[16,8,480]{2,1,0:T(8,128)(2,1)} %param.2) | copy-start | bytes 368644

commit v2 on v0

v2 whole, which is shorter than its diff:
```python
import functools

import jax
import jax.numpy as jnp
from jax import lax
from jax.experimental import pallas as pl
from jax.experimental.pallas import tpu as pltpu
from jax.sharding import PartitionSpec as P

MESH = pl.DeviceIdType.MESH

SHARES = {
    8: [
        [0, 170, 27, 154, 120, 116, 177, 101],
        [85, 0, 85, 114, 57, 177, 170, 166],
        [228, 170, 0, 170, 198, 85, 106, 89],
        [101, 141, 85, 0, 154, 216, 226, 83],
        [135, 198, 57, 101, 0, 170, 27, 154],
        [139, 78, 170, 39, 85, 0, 85, 114],
        [78, 85, 149, 29, 228, 170, 0, 170],
        [154, 89, 166, 172, 101, 141, 85, 0],
    ],
    4: [[0, 3, 5, 9], [12, 0, 6, 10], [10, 9, 0, 3], [6, 5, 12, 0]],
}


def pick(index, values):
    out = jnp.int32(values[0])
    for i, v in enumerate(values[1:], 1):
        out = jnp.where(index == i, jnp.int32(v), out)
    return out


def bit(mask, i):
    return (mask >> i) & 1 == 1


def loop(lo, hi, act):
    def body(i, carry):
        act(i)
        return carry

    lax.fori_loop(lo, hi, body, 0)


def kernel(nb, m_hbm, w_hbm, out_ref, m_own, mt_own, w, rows, cols, gram, red1, red2,
           load_sem, w_sem, plane_send, rows_recv, rows_fwd, cols_recv, cols_send, column_send,
           red1_send, red1_recv, red2_send, red2_recv):
    share = SHARES[nb]
    zs, pairs = nb, nb // 2
    full = (1 << nb) - 1
    even = sum(1 << i for i in range(0, nb, 2))
    p, q = lax.axis_index("band"), lax.axis_index("grow")
    core, chip = q % 2, q // 2
    pair, side = chip // 2, chip % 2
    diag = pair == p
    tile, n = mt_own.shape
    window = w.shape[1]
    pad = window - 2 * tile
    sibling = (p, q + 1 - 2 * core)

    def chip_at(line, chip_to, core_at):
        return (line, 2 * chip_to + core_at)

    beside = chip + 1 - 2 * side

    load_m = pltpu.make_async_copy(m_hbm, m_own, load_sem.at[0])
    load_m.start()
    own_rows = pl.ds(pl.multiple_of(core * tile, 16), tile)
    far = 4 * tile - window
    load_w = pltpu.make_async_copy(w_hbm.at[:, pl.ds(pl.multiple_of(core * far, 128), window)], w.at[own_rows], load_sem.at[1])
    load_w.start()
    give_w = pltpu.make_async_remote_copy(
        src_ref=w_hbm.at[:, pl.ds(pl.multiple_of((1 - core) * far, 128), window)], dst_ref=w.at[own_rows],
        send_sem=w_sem.at[0], recv_sem=w_sem.at[1], device_id=sibling, device_id_type=MESH)

    barrier = pltpu.get_barrier_semaphore()

    def greet(device):
        pl.semaphore_signal(barrier, inc=1, device_id=device, device_id_type=MESH)

    place1 = 2 * p + core

    def plane_device(i):
        return (i // 2, 2 * chip + i % 2)

    loop(1, 2 * nb, lambda i: greet(plane_device((place1 + i) % (2 * nb))))
    loop(1, 2 * zs, lambda i: greet(chip_at(p, (chip + i) % (2 * zs), core)))

    def words_of(line):
        words = []
        for r in range(2):
            v = [sum(share[r * pairs + i][l] << (nb * i) for i in range(pairs)) for l in range(nb)]
            words.append(pick(line, [x - (x >> 31 << 32) for x in v]))
        return words

    def shared(at, words):
        return (jnp.where(at // pairs == 0, words[0], words[1]) >> (nb * (at % pairs))) & full

    def leader(at, line, c):
        return pick((at + pairs - line % pairs) % pairs, [c, 0] if pairs == 2 else [c, 0, 1 - c, 1])

    def straight(at, line, c):
        ahead = (at + pairs - line % pairs) % pairs
        return ((ahead == 1) & (c == 1)) | ((ahead == pairs - 1) & (c == 0))

    def targets(line, words, c, pp, act):
        def one(i):
            at = (line + 1 + i) % nb
            home = at == line
            goes = jnp.where(home, pp % 2 == 1 - c, bit(shared(at, words), pp))
            to = 2 * at + jnp.where(home, 1 - c, leader(at, line, c))

            @pl.when(goes)
            def _():
                act(0, at, to)

            @pl.when(goes & ~home & straight(at, line, c))
            def _():
                act(1, at, 2 * at + 1 - leader(at, line, c))

        loop(0, nb, one)

    own_words = words_of(p)
    here = jnp.where(~diag, shared(pair, own_words), jnp.where(side == core, 0, jnp.where(side == 0, even, full - even)))
    direct = diag | straight(pair, p, core) | (side == leader(pair, p, core))
    leads = direct & ~diag & ~straight(pair, p, core)
    row_mask = jnp.where(diag, 0, shared(pair, own_words))
    to_lines = jnp.int32(0)
    for l in range(nb):
        m = pick(pair, [share[r][l] for r in range(nb)])
        to_lines |= jnp.where((m >> p) & 1 == 1, 1 << l, 0)
    def greet_sender(pp):
        @pl.when(direct & bit(here, pp))
        def _():
            for j in range(2):
                greet((pp, 2 * (2 * p + core) + j))

    loop(0, nb, greet_sender)
    load_m.wait()
    mt_own[...] = m_own[...].T
    shard_words = words_of(pair)

    def count(i, total):
        at = (pair + i) % nb
        one = bit(shared(at, shard_words), p)
        return total + jnp.where(one, jnp.where(straight(at, pair, side), 2, 1), 0)

    n_columns = lax.fori_loop(1, nb, count, jnp.where(p % 2 == 1 - side, 1, 0))
    pl.semaphore_wait(barrier, 4 * nb - 2 + n_columns)
    give_w.start()

    def col_place(pp, c, j):
        return cols.at[pp, pl.ds(pl.multiple_of(pad * c + tile * j, 16), tile)]

    def column_copy(k, at, to):
        return pltpu.make_async_remote_copy(
            src_ref=mt_own, dst_ref=col_place(p, side, core), send_sem=column_send.at[at, k], recv_sem=cols_recv.at[p, core],
            device_id=chip_at(pair, to, side), device_id_type=MESH)

    targets(pair, shard_words, side, p, lambda k, at, to: column_copy(k, at, to).start())

    keeps = diag & (core == side)
    to_diag = pltpu.make_async_remote_copy(
        src_ref=mt_own, dst_ref=col_place(p, side, core), send_sem=plane_send.at[nb], recv_sem=cols_recv.at[p, core],
        device_id=(pair, 2 * chip + side), device_id_type=MESH)

    @pl.when(~keeps)
    def _():
        to_diag.start()

    def row_copy(line):
        return pltpu.make_async_remote_copy(
            src_ref=m_own, dst_ref=rows.at[p, core], send_sem=plane_send.at[line], recv_sem=rows_recv.at[p, core],
            device_id=(line, q), device_id_type=MESH)

    def sends_row(line):
        return bit(to_lines, line) & (line != p) & (line != pair)

    def send_row(i):
        line = (p + i) % nb

        @pl.when(sends_row(line))
        def _():
            row_copy(line).start()

    loop(1, nb, send_row)

    def row_forward(pp, j):
        return pltpu.make_async_remote_copy(
            src_ref=rows.at[pp, j], dst_ref=rows.at[pp, j], send_sem=rows_fwd.at[pp, j], recv_sem=rows_recv.at[pp, j],
            device_id=sibling, device_id_type=MESH)

    @pl.when(bit(row_mask, p))
    def _():
        rows[p, core] = m_own[...]

    @pl.when(keeps)
    def _():
        cols[p, pl.ds(pl.multiple_of(pad * side + tile * core, 16), tile)] = mt_own[...]

    if pad:
        def clear(pp):
            cols[pp, pl.ds(pl.multiple_of(2 * tile * (1 - core), 16), pad)] = jnp.zeros((pad, n), jnp.bfloat16)

        loop(0, nb, clear)
    gram[...] = jnp.zeros_like(gram)

    def share_row(pp):
        @pl.when(bit(row_mask, pp))
        def _():
            @pl.when(pp != p)
            def _():
                row_forward(pp, core).wait_recv()

            row_forward(pp, core).start()

    loop(0, nb, share_row)

    def col_copy(pp, j):
        place = col_place(pp, core, j)
        return pltpu.make_async_remote_copy(
            src_ref=place, dst_ref=place, send_sem=cols_send.at[pp, j], recv_sem=cols_recv.at[pp, j],
            device_id=chip_at(p, beside, core), device_id_type=MESH)

    def receive(pp):
        for j in range(2):
            @pl.when(~(keeps & (pp == p) & (j == core)))
            def _():
                col_copy(pp, j).wait_recv()

    def hand_on(pp):
        @pl.when(bit(here, pp))
        def _():
            receive(pp)
            for j in range(2):
                col_copy(pp, j).start()

    @pl.when(leads)
    def _():
        loop(0, nb, hand_on)

    give_w.wait_recv()
    load_w.wait()
    from_sibling = diag & (core != side)

    def use(pp):
        @pl.when(~leads)
        def _():
            receive(pp)

        @pl.when(keeps)
        def _():
            for j in range(2):
                part = cols[pp, pl.ds(pl.multiple_of(pad * side + tile * j, 16), tile)]
                rows[pp, j] = part.T

                @pl.when(pp % 2 == side)
                def _():
                    row_forward(pp, j).start()

        @pl.when(~keeps)
        def _():
            for j in range(2):
                @pl.when(from_sibling | (j != core))
                def _():
                    row_forward(pp, j).wait_recv()

        t = jnp.dot(w[...], cols[pp], preferred_element_type=jnp.float32)
        high = t.astype(jnp.bfloat16)
        low = (t - high.astype(jnp.float32)).astype(jnp.bfloat16)
        both = jnp.concatenate([high, low], axis=1)
        g = jnp.dot(rows[pp, 0], both[:tile], preferred_element_type=jnp.float32)
        g += jnp.dot(rows[pp, 1], both[tile:], preferred_element_type=jnp.float32)
        gram[...] += g[:, :n] + g[:, n:]

    def use_all(pp):
        @pl.when(keeps | bit(here, pp))
        def _():
            use(pp)

    loop(0, nb, use_all)

    bands = n // 16
    row_id = lax.broadcasted_iota(jnp.int32, gram.shape, 0)
    lane_id = lax.broadcasted_iota(jnp.int32, gram.shape, 1)
    kept = jnp.where(row_id % bands == lane_id % bands, gram[...], 0.0) * jnp.where(keeps, 0.5, 1.0)
    red1[place1] = kept.reshape(16, bands, n).sum(axis=1)

    def plane_copy(other):
        return pltpu.make_async_remote_copy(
            src_ref=red1.at[place1], dst_ref=red1.at[place1], send_sem=red1_send.at[other], recv_sem=red1_recv.at[place1],
            device_id=plane_device(other), device_id_type=MESH)

    def plane_wait(other):
        pltpu.make_async_remote_copy(
            src_ref=red1.at[place1], dst_ref=red1.at[other], send_sem=red1_send.at[other], recv_sem=red1_recv.at[other],
            device_id=plane_device(other), device_id_type=MESH).wait_recv()

    loop(1, 2 * nb, lambda i: plane_copy((place1 + i) % (2 * nb)).start())
    give_w.wait_send()
    targets(pair, shard_words, side, p, lambda k, at, to: column_copy(k, at, to).wait_send())

    @pl.when(~keeps)
    def _():
        to_diag.wait_send()

    def sent(pp):
        @pl.when((pp != p) & sends_row(pp))
        def _():
            row_copy(pp).wait_send()

        @pl.when(bit(row_mask, pp))
        def _():
            row_forward(pp, core).wait_send()

        for j in range(2):
            @pl.when(leads & bit(here, pp))
            def _():
                col_copy(pp, j).wait_send()

            @pl.when(keeps & (pp % 2 == side))
            def _():
                row_forward(pp, j).wait_send()

    loop(0, nb, sent)
    loop(1, 2 * nb, lambda i: plane_wait((place1 + i) % (2 * nb)))
    red2[chip] = red1[...].sum(axis=0)

    def line_copy(other):
        return pltpu.make_async_remote_copy(
            src_ref=red2.at[chip], dst_ref=red2.at[chip], send_sem=red2_send.at[other], recv_sem=red2_recv.at[chip],
            device_id=chip_at(p, other, core), device_id_type=MESH)

    def line_wait(other):
        pltpu.make_async_remote_copy(
            src_ref=red2.at[chip], dst_ref=red2.at[other], send_sem=red2_send.at[other], recv_sem=red2_recv.at[other],
            device_id=chip_at(p, other, core), device_id_type=MESH).wait_recv()

    loop(1, 2 * zs, lambda i: line_copy((chip + i) % (2 * zs)).start())
    loop(1, 2 * zs, lambda i: line_wait((chip + i) % (2 * zs)))
    total = red2[...].sum(axis=0)
    fold = jnp.where(
        lax.broadcasted_iota(jnp.int32, (n, 16), 0) // bands == lax.broadcasted_iota(jnp.int32, (n, 16), 1), 1.0, 0.0)
    s = jnp.dot(total, fold, precision=lax.Precision.HIGHEST, preferred_element_type=jnp.float32)
    s_t = lax.dot_general(fold, total, (((0,), (1,)), ((), ())), precision=lax.Precision.HIGHEST,
                          preferred_element_type=jnp.float32)
    out_ref[...] = -(s + s_t)

    loop(1, 2 * nb, lambda i: plane_copy((place1 + i) % (2 * nb)).wait_send())
    loop(1, 2 * zs, lambda i: line_copy((chip + i) % (2 * zs)).wait_send())


def body(nb, pair_matrices, screened):
    states, bands, tile = pair_matrices.shape
    n = states * bands
    flat = pair_matrices.reshape(n, tile)
    window = -(-2 * tile // 128) * 128
    dma = pltpu.SemaphoreType.DMA
    small = pltpu.VMEM((2 * nb, states, n), jnp.float32)
    return pl.pallas_call(
        functools.partial(kernel, nb),
        out_shape=jax.ShapeDtypeStruct((states, states), jnp.float32),
        in_specs=[pl.BlockSpec(memory_space=pl.ANY)] * 2,
        out_specs=pl.BlockSpec(memory_space=pltpu.VMEM),
        scratch_shapes=[
            pltpu.VMEM((n, tile), jnp.bfloat16),
            pltpu.VMEM((tile, n), jnp.bfloat16),
            pltpu.VMEM((2 * tile, window), jnp.bfloat16),
            pltpu.VMEM((nb, 2, n, tile), jnp.bfloat16),
            pltpu.VMEM((nb, window, n), jnp.bfloat16),
            pltpu.VMEM((n, n), jnp.float32),
            small,
            small,
            dma((2,)), dma((2,)), dma((nb + 1,)), dma((nb, 2)), dma((nb, 2)), dma((nb, 2)), dma((nb, 2)), dma((nb, 2)),
            dma((2 * nb,)), dma((2 * nb,)), dma((2 * nb,)), dma((2 * nb,)),
        ],
        compiler_params=pltpu.CompilerParams(collective_id=0, has_side_effects=True, vmem_limit_bytes=40 * 1024 * 1024),
    )(flat, screened)


def solution(mesh):
    placed = (P(None, "band", "grow"), P("grow", "band"))
    return jax.shard_map(functools.partial(body, mesh.shape["band"]), mesh=mesh, in_specs=placed, out_specs=P(), check_vma=False)
```

time: 478 us -> 65.1 us (0.14)
  waiting for transfers between devices: 317 us -> 0 us
  blocking collectives: 81.4 us -> 0 us
  Pallas kernels: 0 us -> 61.8 us
  matrix products: 32 us -> 0 us
  local copies, waits for them, and re-layouts: 23.9 us -> 3.01 us
  between operations: 13.6 us -> 0.01 us
  starting transfers between devices: 9.72 us -> 0 us
    ppermute x7 -> x0, waiting for transfers between devices: 304 us -> none  [from_behind(): lax.ppermute(x, axis, [(i, (i + by) % devices) for i in range(devices)])]
    psum x1 -> x0, blocking collectives: 81.4 us -> none  [body(): sigma_sum = lax.psum(sigma_sum, ('band', 'grow'))]
    pallas_call x0 -> x1, Pallas kernels: none -> 61.8 us  [body(): pl.pallas_call(functools.partial(kernel, nb), out_shape=jax.ShapeDtypeStr...]
    dot_general x16 -> x0, matrix products: 32 us -> none  [the longest x8 20.2 us: contribute(): jnp.einsum('sbh,tbh->st', partial_x, columns, precision=lax.Precision.HIG...]
    dynamic_slice x1 -> x0, local copies, waits for them, and re-layouts: 18.8 us -> none  [contribute(): lax.dynamic_slice_in_dim(gathered, anchor * panel_width, panel_width, 2)]
    all_gather x1 -> x0, waiting for transfers between devices: 13.3 us -> none  [body(): gathered = lax.all_gather(pair_matrices, 'grow', axis=2, tiled=True)]
    ppermute x7 -> x0, starting transfers between devices: 9.72 us -> none  [from_behind(): lax.ppermute(x, axis, [(i, (i + by) % devices) for i in range(devices)])]
  transfers between devices with their start and end apart: 8 -> 0, of which waited for: 7 -> 0; matrix products, arithmetic and copies ran while one was open for 11% -> 0% of each run, Pallas kernels for 0% -> 0%
where the time goes in v2:
time: 65.1 us; the launch traced here: 64.9 us
  Pallas kernels  61.8 us (95%)
  local copies, waits for them, and re-layouts  3.01 us (5%)
    pallas_call x1, Pallas kernels, body(): pl.pallas_call(functools.partial(kernel, nb), out_shape=jax.ShapeDtypeStr...  61.8 us
    unnamed x5, local copies, waits for them, and re-layouts  3.01 us

profile of v2, /device:TPU:1, one launch (start us, length us, event | category | flops | bytes accessed | tf_op | source)
XLA Modules:
  0.0 64.9 jit_solution(15268608221040850998)
XLA Ops:
  0.0 0.0 copy-start
  0.0 1.5 %copy-done = bf16[480,1920]{1,0:T(8,128)(2,1)S(1)} copy-done((bf16[480,1920]{1,0:T(8,128)(2,1)S(1)}, bf16[480,1920]{1,0:T(8,128)(2,1)}, u32[]{:S(2)}) %copy-start) | copy-done | bytes 1843224
  1.5 0.0 copy-start.1
  1.5 0.9 %copy-done.1 = bf16[16,8,480]{2,1,0:T(8,128)(2,1)S(1)} copy-done((bf16[16,8,480]{2,1,0:T(8,128)(2,1)S(1)}, bf16[16,8,480]{2,1,0:T(8,128)(2,1)}, u32[]{:S(2)}) %copy-start.1) | copy-done | bytes 122904
  2.4 61.8 %shard_map.28 = f32[16,16]{1,0:T(8,128)S(1)} custom-call(bf16[128,480]{1,0:T(8,128)(2,1)S(1)} %bitcast.1, bf16[480,1920]{1,0:T(8,128)(2,1)S(1)} %copy-done), custom_call_target="tpu_custom_call" | custom-call | tf_op jit(solution)/shard_map/pallas_call | solution.py:361
  64.3 0.6 copy.4
Async XLA Ops:
  0.0 1.5 %copy-start = (bf16[480,1920]{1,0:T(8,128)(2,1)S(1)}, bf16[480,1920]{1,0:T(8,128)(2,1)}, u32[]{:S(2)}) copy-start(bf16[480,1920]{1,0:T(8,128)(2,1)} %w_hbm.1) | copy-start | bytes 5529604
  1.5 0.9 %copy-start.1 = (bf16[16,8,480]{2,1,0:T(8,128)(2,1)S(1)}, bf16[16,8,480]{2,1,0:T(8,128)(2,1)}, u32[]{:S(2)}) copy-start(bf16[16,8,480]{2,1,0:T(8,128)(2,1)} %param.2) | copy-start | bytes 368644

commit v3 on v2

--- a/solution.py
+++ b/solution.py
@@ -111,15 +111,21 @@
             goes = jnp.where(home, pp % 2 == 1 - c, bit(shared(at, words), pp))
             to = 2 * at + jnp.where(home, 1 - c, leader(at, line, c))
 
-            @pl.when(goes)
+            both = straight(at, line, c)
+
+            @pl.when(goes & (i < nb) & ~home & ~both)
             def _():
                 act(0, at, to)
 
-            @pl.when(goes & ~home & straight(at, line, c))
+            @pl.when(goes & (i >= nb) & (home | both))
+            def _():
+                act(0, at, to)
+
+            @pl.when(goes & (i >= nb) & ~home & both)
             def _():
                 act(1, at, 2 * at + 1 - leader(at, line, c))
 
-        loop(0, nb, one)
+        loop(0, 2 * nb, one)
 
     own_words = words_of(p)
     here = jnp.where(~diag, shared(pair, own_words), jnp.where(side == core, 0, jnp.where(side == 0, even, full - even)))
@@ -206,17 +212,6 @@
         loop(0, nb, clear)
     gram[...] = jnp.zeros_like(gram)
 
-    def share_row(pp):
-        @pl.when(bit(row_mask, pp))
-        def _():
-            @pl.when(pp != p)
-            def _():
-                row_forward(pp, core).wait_recv()
-
-            row_forward(pp, core).start()
-
-    loop(0, nb, share_row)
-
     def col_copy(pp, j):
         place = col_place(pp, core, j)
         return pltpu.make_async_remote_copy(
@@ -232,13 +227,29 @@
     def hand_on(pp):
         @pl.when(bit(here, pp))
         def _():
-            receive(pp)
             for j in range(2):
+                col_copy(pp, j).wait_recv()
                 col_copy(pp, j).start()
 
+    def near(i):
+        ny = nb // 2
+        step = pick(i // 2, [0, 1, ny - 1, 2][:ny] if ny > 2 else [0, 1])
+        return 2 * ((p // 2 + step) % ny) + (p + i) % 2
+
     @pl.when(leads)
     def _():
-        loop(0, nb, hand_on)
+        loop(0, nb, lambda i: hand_on(near(i)))
+
+    def share_row(pp):
+        @pl.when(bit(row_mask, pp))
+        def _():
+            @pl.when(pp != p)
+            def _():
+                row_forward(pp, core).wait_recv()
+
+            row_forward(pp, core).start()
+
+    loop(0, nb, share_row)
 
     give_w.wait_recv()
     load_w.wait()
@@ -279,7 +290,7 @@
         def _():
             use(pp)
 
-    loop(0, nb, use_all)
+    loop(0, nb, lambda i: use_all(near(i)))
 
     bands = n // 16
     row_id = lax.broadcasted_iota(jnp.int32, gram.shape, 0)

time: 65.1 us -> 57 us (0.88)
  Pallas kernels: 61.8 us -> 53.8 us
    pallas_call x1, Pallas kernels: 61.8 us -> 53.8 us  [body(): pl.pallas_call(functools.partial(kernel, nb), out_shape=jax.ShapeDtypeStr...]
where the time goes in v3:
time: 57 us; the launch traced here: 56.8 us
  Pallas kernels  53.8 us (94%)
  local copies, waits for them, and re-layouts  3.01 us (5%)
    pallas_call x1, Pallas kernels, body(): pl.pallas_call(functools.partial(kernel, nb), out_shape=jax.ShapeDtypeStr...  53.8 us
    unnamed x5, local copies, waits for them, and re-layouts  3.01 us

profile of v3, /device:TPU:1, one launch (start us, length us, event | category | flops | bytes accessed | tf_op | source)
XLA Modules:
  0.0 56.8 jit_solution(2181648342409829559)
XLA Ops:
  0.0 0.0 copy-start
  0.0 1.5 %copy-done = bf16[480,1920]{1,0:T(8,128)(2,1)S(1)} copy-done((bf16[480,1920]{1,0:T(8,128)(2,1)S(1)}, bf16[480,1920]{1,0:T(8,128)(2,1)}, u32[]{:S(2)}) %copy-start) | copy-done | bytes 1843224
  1.5 0.0 copy-start.1
  1.5 0.9 %copy-done.1 = bf16[16,8,480]{2,1,0:T(8,128)(2,1)S(1)} copy-done((bf16[16,8,480]{2,1,0:T(8,128)(2,1)S(1)}, bf16[16,8,480]{2,1,0:T(8,128)(2,1)}, u32[]{:S(2)}) %copy-start.1) | copy-done | bytes 122904
  2.4 53.8 %shard_map.28 = f32[16,16]{1,0:T(8,128)S(1)} custom-call(bf16[128,480]{1,0:T(8,128)(2,1)S(1)} %bitcast.1, bf16[480,1920]{1,0:T(8,128)(2,1)S(1)} %copy-done), custom_call_target="tpu_custom_call" | custom-call | tf_op jit(solution)/shard_map/pallas_call | solution.py:372
  56.2 0.6 %copy.4 = f32[16,16]{1,0:T(8,128)} copy(f32[16,16]{1,0:T(8,128)S(1)} %shard_map.28) | data formatting | bytes 2048
Async XLA Ops:
  0.0 1.5 %copy-start = (bf16[480,1920]{1,0:T(8,128)(2,1)S(1)}, bf16[480,1920]{1,0:T(8,128)(2,1)}, u32[]{:S(2)}) copy-start(bf16[480,1920]{1,0:T(8,128)(2,1)} %w_hbm.1) | copy-start | bytes 5529604
  1.5 0.9 %copy-start.1 = (bf16[16,8,480]{2,1,0:T(8,128)(2,1)S(1)}, bf16[16,8,480]{2,1,0:T(8,128)(2,1)}, u32[]{:S(2)}) copy-start(bf16[16,8,480]{2,1,0:T(8,128)(2,1)} %param.2) | copy-start | bytes 368644

commit v4 on v3

--- a/solution.py
+++ b/solution.py
@@ -104,28 +104,29 @@
         ahead = (at + pairs - line % pairs) % pairs
         return ((ahead == 1) & (c == 1)) | ((ahead == pairs - 1) & (c == 0))
 
-    def targets(line, words, c, pp, act):
+    def targets(line, words, c, pp, part, act):
         def one(i):
-            at = (line + 1 + i) % nb
+            at = (line + 2 * nb - 1 - i) % nb
             home = at == line
             goes = jnp.where(home, pp % 2 == 1 - c, bit(shared(at, words), pp))
             to = 2 * at + jnp.where(home, 1 - c, leader(at, line, c))
 
             both = straight(at, line, c)
 
-            @pl.when(goes & (i < nb) & ~home & ~both)
-            def _():
-                act(0, at, to)
-
-            @pl.when(goes & (i >= nb) & (home | both))
-            def _():
-                act(0, at, to)
-
-            @pl.when(goes & (i >= nb) & ~home & both)
-            def _():
-                act(1, at, 2 * at + 1 - leader(at, line, c))
-
-        loop(0, 2 * nb, one)
+            if part == 0:
+                @pl.when(goes & ~home & ~both)
+                def _():
+                    act(0, at, to)
+            else:
+                @pl.when(goes & (home | both))
+                def _():
+                    act(0, at, to)
+
+                @pl.when(goes & ~home & both)
+                def _():
+                    act(1, at, 2 * at + 1 - leader(at, line, c))
+
+        loop(0, nb, one)
 
     own_words = words_of(p)
     here = jnp.where(~diag, shared(pair, own_words), jnp.where(side == core, 0, jnp.where(side == 0, even, full - even)))
@@ -164,7 +165,15 @@
             src_ref=mt_own, dst_ref=col_place(p, side, core), send_sem=column_send.at[at, k], recv_sem=cols_recv.at[p, core],
             device_id=chip_at(pair, to, side), device_id_type=MESH)
 
-    targets(pair, shard_words, side, p, lambda k, at, to: column_copy(k, at, to).start())
+    def send(k, at, to):
+        column_copy(k, at, to).start()
+
+    def sent_column(k, at, to):
+        column_copy(k, at, to).wait_send()
+
+    targets(pair, shard_words, side, p, 0, send)
+    targets(pair, shard_words, side, p, 0, sent_column)
+    targets(pair, shard_words, side, p, 1, send)
 
     keeps = diag & (core == side)
     to_diag = pltpu.make_async_remote_copy(
@@ -310,7 +319,7 @@
 
     loop(1, 2 * nb, lambda i: plane_copy((place1 + i) % (2 * nb)).start())
     give_w.wait_send()
-    targets(pair, shard_words, side, p, lambda k, at, to: column_copy(k, at, to).wait_send())
+    targets(pair, shard_words, side, p, 1, sent_column)
 
     @pl.when(~keeps)
     def _():
@@ -334,7 +343,6 @@
             def _():
                 row_forward(pp, j).wait_send()
 
-    loop(0, nb, sent)
     loop(1, 2 * nb, lambda i: plane_wait((place1 + i) % (2 * nb)))
     red2[chip] = red1[...].sum(axis=0)
 
@@ -349,6 +357,7 @@
             device_id=chip_at(p, other, core), device_id_type=MESH).wait_recv()
 
     loop(1, 2 * zs, lambda i: line_copy((chip + i) % (2 * zs)).start())
+    loop(0, nb, sent)
     loop(1, 2 * zs, lambda i: line_wait((chip + i) % (2 * zs)))
     total = red2[...].sum(axis=0)
     fold = jnp.where(

time: 57 us -> 56.1 us (0.984)
  Pallas kernels: 53.8 us -> 52.8 us
    pallas_call x1, Pallas kernels: 53.8 us -> 52.8 us  [body(): pl.pallas_call(functools.partial(kernel, nb), out_shape=jax.ShapeDtypeStr...]
where the time goes in v4:
time: 56.1 us; the launch traced here: 55.8 us
  Pallas kernels  52.8 us (94%)
  local copies, waits for them, and re-layouts  3.01 us (5%)
    pallas_call x1, Pallas kernels, body(): pl.pallas_call(functools.partial(kernel, nb), out_shape=jax.ShapeDtypeStr...  52.8 us
    unnamed x5, local copies, waits for them, and re-layouts  3.01 us

profile of v4, /device:TPU:1, one launch (start us, length us, event | category | flops | bytes accessed | tf_op | source)
XLA Modules:
  0.0 55.8 jit_solution(17388209227064846687)
XLA Ops:
  0.0 0.0 copy-start
  0.0 1.5 %copy-done = bf16[480,1920]{1,0:T(8,128)(2,1)S(1)} copy-done((bf16[480,1920]{1,0:T(8,128)(2,1)S(1)}, bf16[480,1920]{1,0:T(8,128)(2,1)}, u32[]{:S(2)}) %copy-start) | copy-done | bytes 1843224
  1.5 0.0 copy-start.1
  1.5 0.9 %copy-done.1 = bf16[16,8,480]{2,1,0:T(8,128)(2,1)S(1)} copy-done((bf16[16,8,480]{2,1,0:T(8,128)(2,1)S(1)}, bf16[16,8,480]{2,1,0:T(8,128)(2,1)}, u32[]{:S(2)}) %copy-start.1) | copy-done | bytes 122904
  2.4 52.8 %shard_map.28 = f32[16,16]{1,0:T(8,128)S(1)} custom-call(bf16[128,480]{1,0:T(8,128)(2,1)S(1)} %bitcast.1, bf16[480,1920]{1,0:T(8,128)(2,1)S(1)} %copy-done), custom_call_target="tpu_custom_call" | custom-call | tf_op jit(solution)/shard_map/pallas_call | solution.py:381
  55.2 0.6 %copy.4 = f32[16,16]{1,0:T(8,128)} copy(f32[16,16]{1,0:T(8,128)S(1)} %shard_map.28) | data formatting | bytes 2048
Async XLA Ops:
  0.0 1.5 %copy-start = (bf16[480,1920]{1,0:T(8,128)(2,1)S(1)}, bf16[480,1920]{1,0:T(8,128)(2,1)}, u32[]{:S(2)}) copy-start(bf16[480,1920]{1,0:T(8,128)(2,1)} %w_hbm.1) | copy-start | bytes 5529604
  1.5 0.9 %copy-start.1 = (bf16[16,8,480]{2,1,0:T(8,128)(2,1)S(1)}, bf16[16,8,480]{2,1,0:T(8,128)(2,1)}, u32[]{:S(2)}) copy-start(bf16[16,8,480]{2,1,0:T(8,128)(2,1)} %param.2) | copy-start | bytes 368644

commit v5 on v4

--- a/solution.py
+++ b/solution.py
@@ -264,7 +264,7 @@
     load_w.wait()
     from_sibling = diag & (core != side)
 
-    def use(pp):
+    def prepare(pp):
         @pl.when(~leads)
         def _():
             receive(pp)
@@ -286,20 +286,39 @@
                 def _():
                     row_forward(pp, j).wait_recv()
 
-        t = jnp.dot(w[...], cols[pp], preferred_element_type=jnp.float32)
+    def multiply(groups):
+        right = jnp.concatenate([cols[pp] for pp in groups], axis=1) if len(groups) > 1 else cols[groups[0]]
+        t = jnp.dot(w[...], right, preferred_element_type=jnp.float32)
         high = t.astype(jnp.bfloat16)
         low = (t - high.astype(jnp.float32)).astype(jnp.bfloat16)
-        both = jnp.concatenate([high, low], axis=1)
-        g = jnp.dot(rows[pp, 0], both[:tile], preferred_element_type=jnp.float32)
-        g += jnp.dot(rows[pp, 1], both[tile:], preferred_element_type=jnp.float32)
-        gram[...] += g[:, :n] + g[:, n:]
-
-    def use_all(pp):
-        @pl.when(keeps | bit(here, pp))
-        def _():
-            use(pp)
-
-    loop(0, nb, lambda i: use_all(near(i)))
+        for i, pp in enumerate(groups):
+            part = slice(i * n, (i + 1) * n)
+            both = jnp.concatenate([high[:, part], low[:, part]], axis=1)
+            g = jnp.dot(rows[pp, 0], both[:tile], preferred_element_type=jnp.float32)
+            g += jnp.dot(rows[pp, 1], both[tile:], preferred_element_type=jnp.float32)
+            gram[...] += g[:, :n] + g[:, n:]
+
+    def use_one(i):
+        pp = near(i)
+
+        @pl.when(bit(here, pp))
+        def _():
+            prepare(pp)
+            multiply([pp])
+
+    def use_two(i):
+        groups = [near(2 * i), near(2 * i + 1)]
+        for pp in groups:
+            prepare(pp)
+        multiply(groups)
+
+    @pl.when(keeps)
+    def _():
+        loop(0, nb // 2, use_two)
+
+    @pl.when(~keeps)
+    def _():
+        loop(0, nb, use_one)
 
     bands = n // 16
     row_id = lax.broadcasted_iota(jnp.int32, gram.shape, 0)

time: 56.1 us -> 56.1 us (level)
  no operation moved by 1% of the time
where the time goes in v5:
time: 56.1 us; the launch traced here: 55.8 us
  Pallas kernels  52.8 us (94%)
  local copies, waits for them, and re-layouts  3.01 us (5%)
    pallas_call x1, Pallas kernels, body(): pl.pallas_call(functools.partial(kernel, nb), out_shape=jax.ShapeDtypeStr...  52.8 us
    unnamed x5, local copies, waits for them, and re-layouts  3.01 us

profile of v5, /device:TPU:1, one launch (start us, length us, event | category | flops | bytes accessed | tf_op | source)
XLA Modules:
  0.0 55.8 jit_solution(18383685700640591342)
XLA Ops:
  0.0 0.0 copy-start
  0.0 1.5 %copy-done = bf16[480,1920]{1,0:T(8,128)(2,1)S(1)} copy-done((bf16[480,1920]{1,0:T(8,128)(2,1)S(1)}, bf16[480,1920]{1,0:T(8,128)(2,1)}, u32[]{:S(2)}) %copy-start) | copy-done | bytes 1843224
  1.5 0.0 copy-start.1
  1.5 0.9 %copy-done.1 = bf16[16,8,480]{2,1,0:T(8,128)(2,1)S(1)} copy-done((bf16[16,8,480]{2,1,0:T(8,128)(2,1)S(1)}, bf16[16,8,480]{2,1,0:T(8,128)(2,1)}, u32[]{:S(2)}) %copy-start.1) | copy-done | bytes 122904
  2.4 52.8 %shard_map.28 = f32[16,16]{1,0:T(8,128)S(1)} custom-call(bf16[128,480]{1,0:T(8,128)(2,1)S(1)} %bitcast.1, bf16[480,1920]{1,0:T(8,128)(2,1)S(1)} %copy-done), custom_call_target="tpu_custom_call" | custom-call | tf_op jit(solution)/shard_map/pallas_call | solution.py:400
  55.2 0.6 %copy.4 = f32[16,16]{1,0:T(8,128)} copy(f32[16,16]{1,0:T(8,128)S(1)} %shard_map.28) | data formatting | bytes 2048
Async XLA Ops:
  0.0 1.5 %copy-start = (bf16[480,1920]{1,0:T(8,128)(2,1)S(1)}, bf16[480,1920]{1,0:T(8,128)(2,1)}, u32[]{:S(2)}) copy-start(bf16[480,1920]{1,0:T(8,128)(2,1)} %w_hbm.1) | copy-start | bytes 5529604
  1.5 0.9 %copy-start.1 = (bf16[16,8,480]{2,1,0:T(8,128)(2,1)S(1)}, bf16[16,8,480]{2,1,0:T(8,128)(2,1)}, u32[]{:S(2)}) copy-start(bf16[16,8,480]{2,1,0:T(8,128)(2,1)} %param.2) | copy-start | bytes 368644

commit v6 on v5

--- a/solution.py
+++ b/solution.py
@@ -157,32 +157,38 @@
     pl.semaphore_wait(barrier, 4 * nb - 2 + n_columns)
     give_w.start()
 
-    def col_place(pp, c, j):
-        return cols.at[pp, pl.ds(pl.multiple_of(pad * c + tile * j, 16), tile)]
-
-    def column_copy(k, at, to):
-        return pltpu.make_async_remote_copy(
-            src_ref=mt_own, dst_ref=col_place(p, side, core), send_sem=column_send.at[at, k], recv_sem=cols_recv.at[p, core],
+    half = tile // 2
+
+    def col_place(pp, c, j, h):
+        return cols.at[pp, pl.ds(pl.multiple_of(pad * c + tile * j + half * h, 16), half)]
+
+    def column_copy(k, at, to, h):
+        return pltpu.make_async_remote_copy(
+            src_ref=mt_own.at[pl.ds(half * h, half)], dst_ref=col_place(p, side, core, h),
+            send_sem=column_send.at[at, 2 * k + h], recv_sem=cols_recv.at[p, 2 * core + h],
             device_id=chip_at(pair, to, side), device_id_type=MESH)
 
     def send(k, at, to):
-        column_copy(k, at, to).start()
+        for h in range(2):
+            column_copy(k, at, to, h).start()
 
     def sent_column(k, at, to):
-        column_copy(k, at, to).wait_send()
+        for h in range(2):
+            column_copy(k, at, to, h).wait_send()
 
     targets(pair, shard_words, side, p, 0, send)
     targets(pair, shard_words, side, p, 0, sent_column)
     targets(pair, shard_words, side, p, 1, send)
 
     keeps = diag & (core == side)
-    to_diag = pltpu.make_async_remote_copy(
-        src_ref=mt_own, dst_ref=col_place(p, side, core), send_sem=plane_send.at[nb], recv_sem=cols_recv.at[p, core],
-        device_id=(pair, 2 * chip + side), device_id_type=MESH)
+    to_diag = [pltpu.make_async_remote_copy(
+        src_ref=mt_own.at[pl.ds(half * h, half)], dst_ref=col_place(p, side, core, h), send_sem=plane_send.at[nb + h],
+        recv_sem=cols_recv.at[p, 2 * core + h], device_id=(pair, 2 * chip + side), device_id_type=MESH) for h in range(2)]
 
     @pl.when(~keeps)
     def _():
-        to_diag.start()
+        for copy in to_diag:
+            copy.start()
 
     def row_copy(line):
         return pltpu.make_async_remote_copy(
@@ -221,24 +227,24 @@
         loop(0, nb, clear)
     gram[...] = jnp.zeros_like(gram)
 
-    def col_copy(pp, j):
-        place = col_place(pp, core, j)
-        return pltpu.make_async_remote_copy(
-            src_ref=place, dst_ref=place, send_sem=cols_send.at[pp, j], recv_sem=cols_recv.at[pp, j],
+    def col_copy(pp, i):
+        place = col_place(pp, core, i // 2, i % 2)
+        return pltpu.make_async_remote_copy(
+            src_ref=place, dst_ref=place, send_sem=cols_send.at[pp, i], recv_sem=cols_recv.at[pp, i],
             device_id=chip_at(p, beside, core), device_id_type=MESH)
 
     def receive(pp):
-        for j in range(2):
-            @pl.when(~(keeps & (pp == p) & (j == core)))
+        for i in range(4):
+            @pl.when(~(keeps & (pp == p) & (i // 2 == core)))
             def _():
-                col_copy(pp, j).wait_recv()
+                col_copy(pp, i).wait_recv()
 
     def hand_on(pp):
         @pl.when(bit(here, pp))
         def _():
-            for j in range(2):
-                col_copy(pp, j).wait_recv()
-                col_copy(pp, j).start()
+            for i in range(4):
+                col_copy(pp, i).wait_recv()
+                col_copy(pp, i).start()
 
     def near(i):
         ny = nb // 2
@@ -342,7 +348,8 @@
 
     @pl.when(~keeps)
     def _():
-        to_diag.wait_send()
+        for copy in to_diag:
+            copy.wait_send()
 
     def sent(pp):
         @pl.when((pp != p) & sends_row(pp))
@@ -356,7 +363,8 @@
         for j in range(2):
             @pl.when(leads & bit(here, pp))
             def _():
-                col_copy(pp, j).wait_send()
+                for h in range(2):
+                    col_copy(pp, 2 * j + h).wait_send()
 
             @pl.when(keeps & (pp % 2 == side))
             def _():
@@ -411,7 +419,7 @@
             pltpu.VMEM((n, n), jnp.float32),
             small,
             small,
-            dma((2,)), dma((2,)), dma((nb + 1,)), dma((nb, 2)), dma((nb, 2)), dma((nb, 2)), dma((nb, 2)), dma((nb, 2)),
+            dma((2,)), dma((2,)), dma((nb + 2,)), dma((nb, 2)), dma((nb, 2)), dma((nb, 4)), dma((nb, 4)), dma((nb, 4)),
             dma((2 * nb,)), dma((2 * nb,)), dma((2 * nb,)), dma((2 * nb,)),
         ],
         compiler_params=pltpu.CompilerParams(collective_id=0, has_side_effects=True, vmem_limit_bytes=40 * 1024 * 1024),

time: 56.1 us -> 56.8 us (1.012)
  Pallas kernels: 52.8 us -> 53.6 us
    pallas_call x1, Pallas kernels: 52.8 us -> 53.6 us  [body(): pl.pallas_call(functools.partial(kernel, nb), out_shape=jax.ShapeDtypeStr...]
where the time goes in v6:
time: 56.8 us; the launch traced here: 56.6 us
  Pallas kernels  53.6 us (94%)
  local copies, waits for them, and re-layouts  3.01 us (5%)
    pallas_call x1, Pallas kernels, body(): pl.pallas_call(functools.partial(kernel, nb), out_shape=jax.ShapeDtypeStr...  53.6 us
    unnamed x5, local copies, waits for them, and re-layouts  3.01 us

profile of v6, /device:TPU:1, one launch (start us, length us, event | category | flops | bytes accessed | tf_op | source)
XLA Modules:
  0.0 56.6 jit_solution(10098314591314937402)
XLA Ops:
  0.0 0.0 copy-start
  0.0 1.5 %copy-done = bf16[480,1920]{1,0:T(8,128)(2,1)S(1)} copy-done((bf16[480,1920]{1,0:T(8,128)(2,1)S(1)}, bf16[480,1920]{1,0:T(8,128)(2,1)}, u32[]{:S(2)}) %copy-start) | copy-done | bytes 1843224
  1.5 0.0 copy-start.1
  1.5 0.9 %copy-done.1 = bf16[16,8,480]{2,1,0:T(8,128)(2,1)S(1)} copy-done((bf16[16,8,480]{2,1,0:T(8,128)(2,1)S(1)}, bf16[16,8,480]{2,1,0:T(8,128)(2,1)}, u32[]{:S(2)}) %copy-start.1) | copy-done | bytes 122904
  2.4 53.6 %shard_map.28 = f32[16,16]{1,0:T(8,128)S(1)} custom-call(bf16[128,480]{1,0:T(8,128)(2,1)S(1)} %bitcast.1, bf16[480,1920]{1,0:T(8,128)(2,1)S(1)} %copy-done), custom_call_target="tpu_custom_call" | custom-call | tf_op jit(solution)/shard_map/pallas_call | solution.py:408
  56.0 0.6 %copy.4 = f32[16,16]{1,0:T(8,128)} copy(f32[16,16]{1,0:T(8,128)S(1)} %shard_map.28) | data formatting | bytes 2048
Async XLA Ops:
  0.0 1.5 %copy-start = (bf16[480,1920]{1,0:T(8,128)(2,1)S(1)}, bf16[480,1920]{1,0:T(8,128)(2,1)}, u32[]{:S(2)}) copy-start(bf16[480,1920]{1,0:T(8,128)(2,1)} %w_hbm.1) | copy-start | bytes 5529604
  1.5 0.9 %copy-start.1 = (bf16[16,8,480]{2,1,0:T(8,128)(2,1)S(1)}, bf16[16,8,480]{2,1,0:T(8,128)(2,1)}, u32[]{:S(2)}) copy-start(bf16[16,8,480]{2,1,0:T(8,128)(2,1)} %param.2) | copy-start | bytes 368644
